TPU v7x, 128 devices: a whole 4x4x4 slice. The times are simulated.
128 devices in a mesh: gx: 4 (over y), gy: 32 (over z, x, core).
Axes of the slice: x: 4, y: 4, z: 4, core: 2. Of those that a mesh axis runs over, the one named last changes fastest.
Arguments:
- fields: float32 [10, 64, 2048, 128], P(None, 'gx', 'gy'), may hold values from -6 to 6
- diffusivity: float32 [10], replicated, may hold values from 0.03 to 0.12
- decay_rates: float32 [10], replicated, may hold values from 0.3 to 1
- reaction_matrix: float32 [10, 10], replicated, may hold values from -1 to 1
- owner_index: int32 [4, 32768, 1], P('gx', 'gy'), may hold values from 0 to 31, as said below
- flame_flag: int32 [4, 32768, 1], P('gx', 'gy'), may hold values from 0 to 1, as said below
Outputs:
- new_fields: float32 [10, 64, 2048, 128], P(None, 'gx', 'gy')
- owner_heat: float32 [4, 32], P('gx', 'gy')
Inputs may be any that keep to these rules, and one draw needn't show every extreme that they name: `flame_flag`: each device holds exactly 256 or 32 flame blocks; in each index of gx exactly 4 devices along gy, consecutive with wraparound from a drawn start, hold 256. `owner_index`: the flame blocks of one index of gx, taken in order of device and then block, are dealt to owners in turn from a drawn first owner; so one device names each owner for at most 8 of its flame blocks and each owner receives at most 60 flame blocks, both bounds reached on every draw; a block outside the flame names its own device's index along gy.
All inputs are finite; a program needn't handle non-finite values.
Results may differ from a plain program's by a relative error of at most 0.0003.
Values sent between devices are 32-bit elements; how exact they have to be, the bound alone decides.
A program may use at most 128 MiB of HBM per device.

v0:
```python
import functools
import math

import jax
import jax.numpy as jnp
from jax import lax
from jax.experimental import pallas as pl
from jax.experimental.pallas import tpu as pltpu
from jax.sharding import PartitionSpec as P

H_STEP = 0.2
FLAME_SUB = 10
COMP = 10
CX, CY, CZ = 16, 64, 128
CH = CX * CY
FMAX = 256
RMAX = 60

F32, BF16 = jnp.float32, jnp.bfloat16
MESH = pl.DeviceIdType.MESH
VMEM = pl.BlockSpec(memory_space=pltpu.VMEM)
SMEM = pl.BlockSpec(memory_space=pltpu.SMEM)
ANY = pl.BlockSpec(memory_space=pl.ANY)
LIMIT = 56 << 20


def split(values):
    high = values.astype(BF16)
    low = (values - high.astype(F32)).astype(BF16)
    return high, low


def halo_kernel(n_gx, n_gy, fields, taps, diff, out, ext, mid, res, in_sem, send, recv, out_sem):
    gx, gy = lax.axis_index("gx"), lax.axis_index("gy")
    xm, xp = lax.rem(gx + n_gx - 1, n_gx), lax.rem(gx + 1, n_gx)
    ym, yp = lax.rem(gy + n_gy - 1, n_gy), lax.rem(gy + 1, n_gy)
    load = pltpu.make_async_copy(fields, ext.at[:, pl.ds(2, CX), pl.ds(8, CY), :], in_sem)
    load.start()
    targets = [
        (xp, gy), (xm, gy), (gx, yp), (gx, ym), (xp, yp), (xp, ym), (xm, yp), (xm, ym),
    ]
    barrier = pltpu.get_barrier_semaphore()
    for target in targets:
        pl.semaphore_signal(barrier, inc=1, device_id=target, device_id_type=MESH)
    pl.semaphore_wait(barrier, 8)
    ranges = [
        ((CX - 2, 2), (0, CY), (0, 8)),
        ((0, 2), (0, CY), (CX + 2, 8)),
        ((0, CX), (CY - 8, 8), (2, 0)),
        ((0, CX), (0, 8), (2, CY + 8)),
        ((CX - 1, 1), (CY - 8, 8), (1, 0)),
        ((CX - 1, 1), (0, 8), (1, CY + 8)),
        ((0, 1), (CY - 8, 8), (CX + 2, 0)),
        ((0, 1), (0, 8), (CX + 2, CY + 8)),
    ]
    copies = []
    for number, (target, (xs, ys, (dx, dy))) in enumerate(zip(targets, ranges)):
        copies.append(
            pltpu.make_async_remote_copy(
                src_ref=fields.at[:, pl.ds(*xs), pl.ds(*ys), :],
                dst_ref=ext.at[:, pl.ds(dx, xs[1]), pl.ds(dy, ys[1]), :],
                send_sem=send.at[number],
                recv_sem=recv.at[number],
                device_id=target,
                device_id_type=MESH,
            )
        )
    for number in (0, 1, 2, 3, 4, 5, 6, 7):
        copies[number].start()
    load.wait()

    def first(c, x, count):
        d = diff[c]
        shape = (count * 80, CZ)
        v = ext[c, pl.ds(x, count)].reshape(shape)
        near = ext[c, pl.ds(x - 1, count)].reshape(shape) + ext[c, pl.ds(x + 1, count)].reshape(shape)
        near = near + pltpu.roll(v, 1, 0) + pltpu.roll(v, shape[0] - 1, 0)
        near = near + jnp.dot(
            jnp.concatenate(split(v), axis=1), taps[...], preferred_element_type=F32
        )
        mid[c, pl.ds(x - 1, count)] = (v + d * near).reshape(count, 80, CZ)

    def second(c, x, count):
        d = diff[c]
        shape = (count * 80, CZ)
        v = mid[c, pl.ds(x + 1, count)].reshape(shape)
        near = mid[c, pl.ds(x, count)].reshape(shape) + mid[c, pl.ds(x + 2, count)].reshape(shape)
        near = near + pltpu.roll(v, 1, 0) + pltpu.roll(v, shape[0] - 1, 0)
        near = near + jnp.dot(
            jnp.concatenate(split(v), axis=1), taps[...], preferred_element_type=F32
        )
        res[c, pl.ds(x, count)] = (v + d * near).reshape(count, 80, CZ)[:, 8 : 8 + CY]

    def clear(ref, xs, ys):
        @pl.loop(0, COMP)
        def _(c):
            ref[c, pl.ds(*xs), pl.ds(*ys), :] = jnp.zeros((xs[1], ys[1], CZ), F32)

    def edges(ref, xs):
        @pl.when(gy == 0)
        def _():
            clear(ref, xs, (0, 8))

        @pl.when(gy == n_gy - 1)
        def _():
            clear(ref, xs, (CY + 8, 8))

    copies[2].wait_recv()
    copies[3].wait_recv()
    edges(ext, (2, CX))

    @pl.loop(0, COMP)
    def _(c):
        first(c, 3, 7)
        first(c, 10, 7)

    edges(mid, (2, CX - 2))

    @pl.loop(0, COMP)
    def _(c):
        second(c, 2, 6)
        second(c, 8, 6)
        pltpu.make_async_copy(
            res.at[c, pl.ds(2, CX - 4)], out.at[c, pl.ds(2, CX - 4)], out_sem.at[c]
        ).start()

    for number in (0, 1, 4, 5, 6, 7):
        copies[number].wait_recv()
    edges(ext, (1, 1))
    edges(ext, (CX + 2, 1))

    @pl.when(gx == 0)
    def _():
        clear(ext, (0, 2), (0, CY + 16))

    @pl.when(gx == n_gx - 1)
    def _():
        clear(ext, (CX + 2, 2), (0, CY + 16))

    @pl.loop(0, COMP)
    def _(c):
        first(c, 1, 2)
        first(c, CX + 1, 2)

    edges(mid, (1, 1))
    edges(mid, (CX, 1))

    @pl.when(gx == 0)
    def _():
        clear(mid, (0, 1), (0, CY + 16))

    @pl.when(gx == n_gx - 1)
    def _():
        clear(mid, (CX + 1, 1), (0, CY + 16))

    @pl.loop(0, COMP)
    def _(c):
        second(c, 0, 2)
        second(c, CX - 2, 2)
        pltpu.make_async_copy(
            res.at[c, pl.ds(0, 2)], out.at[c, pl.ds(0, 2)], out_sem.at[COMP + c]
        ).start()
        pltpu.make_async_copy(
            res.at[c, pl.ds(CX - 2, 2)], out.at[c, pl.ds(CX - 2, 2)], out_sem.at[2 * COMP + c]
        ).start()

    for copy in copies:
        copy.wait_send()

    @pl.loop(0, COMP)
    def _(c):
        pltpu.make_async_copy(
            res.at[c, pl.ds(2, CX - 4)], out.at[c, pl.ds(2, CX - 4)], out_sem.at[c]
        ).wait()
        pltpu.make_async_copy(
            res.at[c, pl.ds(0, 2)], out.at[c, pl.ds(0, 2)], out_sem.at[COMP + c]
        ).wait()
        pltpu.make_async_copy(
            res.at[c, pl.ds(CX - 2, 2)], out.at[c, pl.ds(CX - 2, 2)], out_sem.at[2 * COMP + c]
        ).wait()


def sigmoid(x):
    return 0.5 * jnp.tanh(0.5 * x) + 0.5


def substep(state, matrix, inverse):
    high, low = split(state)
    r = jnp.dot(matrix, jnp.concatenate([high, low, high], axis=0), preferred_element_type=F32)
    last = state[72:80]
    base = last * inverse[72:80]
    g0 = sigmoid(last)
    g1 = sigmoid(base + g0 * r[240:248])
    g2 = sigmoid(base + g1 * (r[72:80] + g0 * r[248:256]))
    rows = []
    for c in range(COMP):
        at = 8 * c
        inner = r[80 + at : 88 + at] + g0 * r[160 + at : 168 + at]
        rows.append(state[at : at + 8] * inverse[at : at + 8] + g2 * (r[at : at + 8] + g1 * inner))
    return rows


CHUNK = 128


def chem_kernel(u2, matrix, inverse, index, count, owners, out, terms, uv, ov, cur, start_t, in_sem, out_sem):
    for k in range(CH // CHUNK):
        pltpu.make_async_copy(
            u2.at[:, pl.ds(k * CHUNK, CHUNK), :], uv.at[:, pl.ds(k * CHUNK, CHUNK), :], in_sem.at[k]
        ).start()
    inv = inverse[...]
    inv = jnp.concatenate([inv, inv], axis=1)

    @pl.loop(0, CH // CHUNK)
    def _(k):
        part = pl.ds(pl.multiple_of(k * CHUNK, CHUNK), CHUNK)
        pltpu.make_async_copy(u2.at[:, part, :], uv.at[:, part, :], in_sem.at[k]).wait()
        for t in range(CHUNK // 16):
            def group(w):
                at = pl.multiple_of(k * CHUNK + t * 16 + w * 8, 8)
                return jnp.concatenate([uv[c, pl.ds(at, 8), :] for c in range(COMP)], axis=0)

            rows = substep(jnp.concatenate([group(0), group(1)], axis=1), matrix[...], inv)
            for w in range(2):
                at = pl.multiple_of(k * CHUNK + t * 16 + w * 8, 8)
                for c in range(COMP):
                    ov[c, pl.ds(at, 8), :] = rows[c][:, w * CZ : (w + 1) * CZ]

    @pl.loop(0, FMAX // 8)
    def _(g):
        for r in range(8):
            at = index[g * 8 + r]
            for c in range(COMP):
                cur[g, pl.ds(c * 8 + r, 1), :] = uv[c, pl.ds(at, 1), :]
        start_t[g] = cur[g, 72:80, :]

    @pl.loop(0, FLAME_SUB)
    def _(s):
        for t in range(FMAX // 16):
            rows = substep(
                jnp.concatenate([cur[2 * t], cur[2 * t + 1]], axis=1), matrix[...], inv
            )
            new = jnp.concatenate(rows, axis=0)
            cur[2 * t] = new[:, :CZ]
            cur[2 * t + 1] = new[:, CZ:]

    gain = (cur[:, 72:80, :] - start_t[...]).reshape(FMAX, CZ)
    onehot = (lax.broadcasted_iota(jnp.int32, (32, FMAX), 0) == owners[...]).astype(BF16)
    high, low = split(gain)
    total = jnp.dot(onehot, high, preferred_element_type=F32)
    total = total + jnp.dot(onehot, low, preferred_element_type=F32)
    terms[...] = jnp.broadcast_to(total[:, None, :], (32, 8, CZ))

    @pl.loop(0, count[0] // 8)
    def _(g):
        for r in range(8):
            at = index[g * 8 + r]
            for c in range(COMP):
                ov[c, pl.ds(at, 1), :] = cur[g, pl.ds(c * 8 + r, 1), :]

    copy = pltpu.make_async_copy(ov, out, out_sem)
    copy.start()
    copy.wait()


def heat_kernel(n_gy, terms, out, got, send, recv):
    gx, gy = lax.axis_index("gx"), lax.axis_index("gy")
    barrier = pltpu.get_barrier_semaphore()

    @pl.loop(1, n_gy)
    def _(k):
        pl.semaphore_signal(
            barrier, inc=1, device_id=(gx, lax.rem(gy + k, n_gy)), device_id_type=MESH
        )

    pl.semaphore_wait(barrier, n_gy - 1)

    def copy(k):
        other = lax.rem(gy + k, n_gy)
        return pltpu.make_async_remote_copy(
            src_ref=terms.at[other],
            dst_ref=got.at[k],
            send_sem=send.at[k],
            recv_sem=recv.at[k],
            device_id=(gx, other),
            device_id_type=MESH,
        )

    @pl.loop(1, n_gy)
    def _(k):
        copy(k).start()

    got[0] = terms[gy]

    @pl.loop(1, n_gy)
    def _(k):
        copy(k).wait()

    total = jnp.sum(got[:, 0, :], axis=0, keepdims=True)
    out[...] = jnp.sum(total, axis=1, keepdims=True) * (1.0 / math.sqrt(CZ) / math.sqrt(RMAX))


def per_device(n_gx, n_gy, fields, diffusivity, decay_rates, reaction_matrix, owner_index, flame_flag):
    flags = flame_flag.reshape(CH)
    owners = owner_index.reshape(CH)
    rank = jnp.where(flags > 0, jnp.cumsum(flags) - flags, -1)
    count = jnp.sum(flags).reshape(1)
    slots = jnp.arange(FMAX, dtype=jnp.int32)
    code = owners * CH + jnp.arange(CH, dtype=jnp.int32)
    picked = jnp.sum(jnp.where(rank[None, :] == slots[:, None], code[None, :] + 1, 0), axis=1) - 1
    index = jnp.where(picked >= 0, picked % CH, 0)
    slot_owner = jnp.where(picked >= 0, picked // CH, -1).reshape(1, FMAX)
    exact = lax.Precision.HIGHEST
    inv = 1.0 / (1.0 + H_STEP * decay_rates)
    m1 = H_STEP * reaction_matrix * inv[:, None]
    m2 = jnp.dot(m1, m1, precision=exact)
    m3 = jnp.dot(m2, m1, precision=exact)
    every = jnp.concatenate(
        [m1 * inv[None, :], m2 * inv[None, :], m3, m1[9:10], m2[9:10]], axis=0
    )
    high = lax.reduce_precision(every, 8, 7)
    low = lax.reduce_precision(every - high, 8, 7)
    eye = jnp.eye(8, dtype=F32)
    stacked = jnp.concatenate([high, high, low], axis=1)
    matrix = (stacked[:, None, :, None] * eye[None, :, None, :]).reshape(256, 240).astype(BF16)
    inverse = jnp.broadcast_to(jnp.repeat(inv, 8)[:, None], (80, CZ))
    z = jnp.arange(CZ)
    gap = jnp.abs(z[:, None] - z[None, :])
    tap = jnp.where(gap == 0, -6.0, jnp.where(gap == 1, 1.0, 0.0))
    taps = jnp.concatenate([tap, tap], axis=0).astype(BF16)

    shape = (COMP, CX, CY, CZ)
    dma = pltpu.SemaphoreType.DMA
    u2 = pl.pallas_call(
        functools.partial(halo_kernel, n_gx, n_gy),
        out_shape=jax.ShapeDtypeStruct(shape, F32),
        in_specs=[ANY, VMEM, SMEM],
        out_specs=ANY,
        scratch_shapes=[
            pltpu.VMEM((COMP, CX + 4, CY + 16, CZ), F32),
            pltpu.VMEM((COMP, CX + 2, CY + 16, CZ), F32),
            pltpu.VMEM(shape, F32),
            dma,
            dma((8,)),
            dma((8,)),
            dma((3 * COMP,)),
        ],
        compiler_params=pltpu.CompilerParams(
            collective_id=0, has_side_effects=True, vmem_limit_bytes=LIMIT
        ),
        name="halo_diffuse",
    )(fields, taps, diffusivity)
    merged, terms = pl.pallas_call(
        chem_kernel,
        out_shape=(
            jax.ShapeDtypeStruct((COMP, CH, CZ), F32),
            jax.ShapeDtypeStruct((32, 8, CZ), F32),
        ),
        in_specs=[ANY, VMEM, VMEM, SMEM, SMEM, VMEM],
        out_specs=(ANY, VMEM),
        scratch_shapes=[
            pltpu.VMEM((COMP, CH, CZ), F32),
            pltpu.VMEM((COMP, CH, CZ), F32),
            pltpu.VMEM((FMAX // 8, 80, CZ), F32),
            pltpu.VMEM((FMAX // 8, 8, CZ), F32),
            dma((CH // CHUNK,)),
            dma,
        ],
        compiler_params=pltpu.CompilerParams(vmem_limit_bytes=LIMIT),
        name="chemistry",
    )(u2.reshape(COMP, CH, CZ), matrix, inverse, index, count, slot_owner)
    heat = pl.pallas_call(
        functools.partial(heat_kernel, n_gy),
        out_shape=jax.ShapeDtypeStruct((1, 1), F32),
        in_specs=[VMEM],
        out_specs=VMEM,
        scratch_shapes=[pltpu.VMEM((n_gy, 8, CZ), F32), dma((n_gy,)), dma((n_gy,))],
        compiler_params=pltpu.CompilerParams(
            collective_id=1, has_side_effects=True, vmem_limit_bytes=LIMIT
        ),
        name="owner_sum",
    )(terms)
    return merged.reshape(shape), heat


def solution(mesh):
    return jax.shard_map(
        functools.partial(per_device, mesh.shape["gx"], mesh.shape["gy"]),
        mesh=mesh,
        in_specs=(
            P(None, "gx", "gy", None),
            P(),
            P(),
            P(),
            P("gx", "gy", None),
            P("gx", "gy", None),
        ),
        out_specs=(P(None, "gx", "gy", None), P("gx", "gy")),
        check_vma=False,
    )
```

profile of v0, /device:TPU:1, one launch (start us, length us, event | category | flops | bytes accessed | tf_op | source)
XLA Modules:
  0.0 78.2 jit_solution(18056137165380681096)
XLA Ops:
  0.6 1.3 %reduce_sum.19 = s32[]{:T(128)} reduce(s32[1,1024,1]{1,2,0:T(1,128)} %param.11, s32[]{:T(128)} %constant.20.clone.1), dimensions={0,1,2}, to_apply=%region_3.4 | reduce | flops 1023 | bytes 4104 | tf_op jit(solution)/shard_map/reduce_sum | solution.py:307
  2.0 0.7 broadcast_multiply_fusion.4
  2.6 1.0 %reduce-window.9 = s32[8,128]{1,0:T(8,128)S(1)} reduce-window(s32[8,128]{1,0:T(8,128)} %bitcast.20, s32[]{:T(128)} %constant.20.clone.1), window={size=1x128 pad=0_0x127_0}, to_apply=%region_0.0 | reduce-window | flops 130048 | bytes 8196 | tf_op jit(solution)/shard_map/reduce-window
  3.6 0.1 slice.15
  3.7 0.1 slice_reduce_fusion
  3.8 0.7 broadcast_multiply_fusion.3
  4.5 0.8 fusion.2
  5.3 0.2 select_reduce_fusion
  5.5 0.6 broadcast_add_fusion
  6.0 0.6 compare_select_fusion.owners
  6.6 0.1 broadcast_in_dim.54
  6.7 0.1 broadcast_in_dim.55
  6.8 0.8 broadcast_multiply_fusion.1
  7.6 0.1 broadcast_multiply_fusion
  7.7 0.1 fusion.6
  7.8 0.3 concatenate.11
  8.1 0.1 pad_maximum_fusion.1
  8.2 0.1 copy.13
  8.3 0.6 pad_maximum_fusion.taps
  9.0 0.7 broadcast_in_dim.56.inverse
  9.6 0.4 multiply_convert_fusion
  10.0 3.3 %convert_element_type.15 = bf16[256,240]{0,1:T(8,128)(2,1)S(1)} reshape(bf16[32,8,30,8]{1,0,3,2:T(8,128)(2,1)S(1)} %multiply_convert_fusion) | data formatting | bytes 245760 | tf_op jit(solution)/shard_map/convert_element_type | solution.py:325
  13.3 0.8 copy.14.matrix
  14.1 28.5 %halo_diffuse.1 = f32[10,16,64,128]{3,2,1,0:T(8,128)} custom-call(f32[10,16,64,128]{3,2,1,0:T(8,128)} %fields.1, bf16[256,128]{1,0:T(8,128)(2,1)} %pad_maximum_fusion.taps, f32[10]{0:T(128)} %diff.1), custom_call_target="tpu_custom_call" | custom-call | tf_op jit(solution)/shard_map/halo_diffuse/pallas_call | solution.py:334
  42.5 19.9 %chemistry.1 = (f32[10,1024,128]{2,1,0:T(8,128)}, f32[32,8,128]{2,1,0:T(8,128)}) custom-call(f32[10,1024,128]{2,1,0:T(8,128)} %bitcast.19, bf16[256,240]{1,0:T(8,128)(2,1)} %copy.14.matrix, f32[80,128]{1,0:T(8,128)} %broadcast_in_dim.56.inverse, s32[256]{0:T(256)} %get-tuple-element.13.index, s32[1]{0:T(128)} %bitcast.5.count, ...), custom_call_target="tpu_custom_call" | custom-call | tf_op jit(solution)/shard_map/chemistry/pallas_call | solution.py:353
  62.5 13.9 %owner_sum.1 = f32[1,1]{1,0:T(1,128)} custom-call(f32[32,8,128]{2,1,0:T(8,128)} %get-tuple-element.5.terms), custom_call_target="tpu_custom_call" | custom-call | tf_op jit(solution)/shard_map/owner_sum/pallas_call | solution.py:372
  (6 shorter events, 0.1 us)
where the time goes:
time: 78.6 us; the launch traced here: 78.2 us
  Pallas kernels  62.3 us (79%)
  other arithmetic  7.72 us (10%)
  local copies, waits for them, and re-layouts  5.41 us (7%)
  between operations  2.5 us (3%)
    pallas_call x1, Pallas kernels, per_device(): pl.pallas_call(functools.partial(halo_kernel, n_gx, n_gy), out_shape=jax....  28.5 us
    pallas_call x1, Pallas kernels, per_device(): pl.pallas_call(chem_kernel, out_shape=(jax.ShapeDtypeStruct((COMP, CH, CZ...  19.9 us
    pallas_call x1, Pallas kernels, per_device(): pl.pallas_call(functools.partial(heat_kernel, n_gy), out_shape=jax.ShapeD...  13.9 us
    convert_element_type x2, local copies, waits for them, and re-layouts, per_device(): (stacked[:, None, :, None] * eye[None, :, None, :]).reshape(256, 240)  4.02 us

commit v1 on v0

v1 whole, which is shorter than its diff:
```python
import functools
import math

import jax
import jax.numpy as jnp
from jax import lax
from jax.experimental import pallas as pl
from jax.experimental.pallas import tpu as pltpu
from jax.sharding import PartitionSpec as P

H_STEP = 0.2
FLAME_SUB = 10
COMP = 10
CX, CY, CZ = 16, 64, 128
CH = CX * CY
FMAX = 256
RMAX = 60
EARLY = 160
LATE = 96
CHUNK = 128
COOL_EACH = 6

F32, BF16 = jnp.float32, jnp.bfloat16
MESH = pl.DeviceIdType.MESH
VMEM = pl.BlockSpec(memory_space=pltpu.VMEM)
SMEM = pl.BlockSpec(memory_space=pltpu.SMEM)
ANY = pl.BlockSpec(memory_space=pl.ANY)
LIMIT = 56 << 20


def split(values):
    high = values.astype(BF16)
    low = (values - high.astype(F32)).astype(BF16)
    return high, low


def tables(reaction, decay, flags, owners, taps, matrix, inverse, lists, late, pad):
    exact = lax.Precision.HIGHEST
    iota = lax.broadcasted_iota
    one = jnp.float32(1.0)
    gap = jnp.abs((iota(jnp.int32, (2 * CZ, CZ), 0) & (CZ - 1)) - iota(jnp.int32, (2 * CZ, CZ), 1))
    taps[...] = jnp.where(gap == 0, -6.0, jnp.where(gap == 1, 1.0, 0.0)).astype(BF16)

    shares = [one / (one + H_STEP * jnp.full((8, CZ), decay[c], F32)) for c in range(COMP)]
    for c in range(COMP):
        inverse[pl.ds(8 * c, 8), :] = shares[c]
    sub, lane = iota(jnp.int32, (16, CZ), 0), iota(jnp.int32, (16, CZ), 1)
    by_row = jnp.zeros((16, CZ), F32)
    by_lane = jnp.zeros((16, CZ), F32)
    for c in range(COMP):
        share = jnp.concatenate([shares[c], shares[c]], axis=0)
        by_row = jnp.where(sub == c, share, by_row)
        by_lane = jnp.where(lane == c, share, by_lane)
    pad[...] = jnp.zeros((CZ, CZ), F32)
    pad[0:COMP, 0:COMP] = reaction[...]
    m1 = H_STEP * pad[0:16, :] * by_row
    pad[0:16, :] = m1
    full = pad[...]
    m2 = jnp.dot(m1, full, precision=exact, preferred_element_type=F32)
    m3 = jnp.dot(m2, full, precision=exact, preferred_element_type=F32)
    d1, d2 = m1 * by_lane, m2 * by_lane
    every = jnp.concatenate([d1, d2, m3, m1, m2], axis=0)
    high, low = split(every)
    row = iota(jnp.int32, (256, 80), 0) >> 3
    source = row + 6 * (row >= 10).astype(jnp.int32) + 6 * (row >= 20).astype(jnp.int32)
    source = jnp.where(row == 30, 48 + 9, jnp.where(row == 31, 64 + 9, source))
    up = (source == iota(jnp.int32, (256, 80), 1)).astype(BF16)
    column = iota(jnp.int32, (CZ, 240), 1)
    third = (column >= 80).astype(jnp.int32) + (column >= 160).astype(jnp.int32)
    across = (((column - 80 * third) >> 3) == iota(jnp.int32, (CZ, 240), 0)).astype(BF16)
    spread = [
        jnp.dot(
            jnp.dot(up, part, preferred_element_type=F32).astype(BF16),
            across,
            preferred_element_type=F32,
        )
        for part in (high, low)
    ]
    r, n = iota(jnp.int32, (256, 240), 0), iota(jnp.int32, (256, 240), 1)
    value = jnp.where(n < 160, spread[0], spread[1])
    matrix[...] = jnp.where((r & 7) == (n & 7), value, 0.0).astype(BF16)

    flame = flags[...].astype(F32)
    upper = (iota(jnp.int32, (CZ, CZ), 0) <= iota(jnp.int32, (CZ, CZ), 1)).astype(BF16)
    count = jnp.dot(flame.astype(BF16), upper, preferred_element_type=F32)
    total = jnp.dot(flame.astype(BF16), jnp.ones((CZ, CZ), BF16), preferred_element_type=F32)
    inner = jnp.zeros((1, CZ), F32)
    keys = [None] * 8
    for k in range(1, 7):
        keys[k] = count[k : k + 1] - 1.0 + inner
        inner = inner + total[k : k + 1]
    rest = jnp.maximum(inner - EARLY, 0.0)
    keys[0] = count[0:1] - 1.0 + rest
    keys[7] = count[7:8] - 1.0 + rest + total[0:1]
    keys = jnp.concatenate(keys, axis=0)
    which = iota(jnp.int32, (8, CZ), 0)
    outer = (which == 0) | (which == 7)
    on = flame > 0.0
    early = jnp.where(on & ~outer & (keys < EARLY), keys, -1.0)
    after = jnp.where(outer, keys, keys - EARLY)
    after = jnp.where(on & (after >= 0.0), after, -1.0)
    slot = iota(jnp.int32, (FMAX, CZ), 0).astype(F32)
    label = iota(jnp.int32, (8, CZ), 0)
    here = iota(jnp.int32, (8, CZ), 1).astype(F32)
    owner = owners[...].astype(F32)

    def listed(key):
        got = jnp.zeros((8, FMAX), F32)
        for k in range(8):
            hit = (slot == key[k : k + 1]).astype(BF16)
            facts = jnp.where(label == 0, here, jnp.where(label == 1, owner[k : k + 1], 1.0))
            facts = jnp.where(label == 3, float(k), facts)
            got = got + lax.dot_general(
                facts.astype(BF16), hit, (((1,), (1,)), ((), ())), preferred_element_type=F32
            )
        valid = got[2:3]
        index = got[3:4] * float(CZ) + got[0:1] + (1.0 - valid) * float(CZ)
        who = got[1:2] + valid - 1.0
        number = jnp.sum(valid, axis=1, keepdims=True) + jnp.zeros((1, FMAX), F32)
        zero = jnp.zeros((1, FMAX), F32)
        rows = [index, who, number, zero, zero, zero, zero, zero]
        return jnp.concatenate(rows, axis=0).astype(jnp.int32)

    lists[...] = listed(early)
    late[...] = listed(after)


def halo_kernel(
    n_gx, n_gy, fields, diff, reaction, decay, flags, owners,
    out, hot, gain, matrix, inverse, lists, late,
    ext, mid, res, taps, pad, where, first_t, in_sem, send, recv, out_sem, list_sem,
):
    gx, gy = lax.axis_index("gx"), lax.axis_index("gy")
    xm, xp = lax.rem(gx + n_gx - 1, n_gx), lax.rem(gx + 1, n_gx)
    ym, yp = lax.rem(gy + n_gy - 1, n_gy), lax.rem(gy + 1, n_gy)
    load = pltpu.make_async_copy(fields, ext.at[:, pl.ds(2, CX), pl.ds(8, CY), :], in_sem)
    load.start()
    targets = [
        (xp, gy), (xm, gy), (gx, yp), (gx, ym), (xp, yp), (xp, ym), (xm, yp), (xm, ym),
    ]
    barrier = pltpu.get_barrier_semaphore()
    for target in targets:
        pl.semaphore_signal(barrier, inc=1, device_id=target, device_id_type=MESH)
    pl.semaphore_wait(barrier, 8)
    ranges = [
        ((CX - 2, 2), (0, CY), (0, 8)),
        ((0, 2), (0, CY), (CX + 2, 8)),
        ((0, CX), (CY - 2, 2), (2, 6)),
        ((0, CX), (0, 2), (2, CY + 8)),
        ((CX - 1, 1), (CY - 1, 1), (1, 7)),
        ((CX - 1, 1), (0, 1), (1, CY + 8)),
        ((0, 1), (CY - 1, 1), (CX + 2, 7)),
        ((0, 1), (0, 1), (CX + 2, CY + 8)),
    ]
    copies = []
    for number, (target, (xs, ys, (dx, dy))) in enumerate(zip(targets, ranges)):
        copies.append(
            pltpu.make_async_remote_copy(
                src_ref=fields.at[:, pl.ds(*xs), pl.ds(*ys), :],
                dst_ref=ext.at[:, pl.ds(dx, xs[1]), pl.ds(dy, ys[1]), :],
                send_sem=send.at[number],
                recv_sem=recv.at[number],
                device_id=target,
                device_id_type=MESH,
            )
        )
    for number in (0, 1, 2, 3, 4, 5, 6, 7):
        copies[number].start()
    tables(reaction, decay, flags, owners, taps, matrix, inverse, lists, late, pad)
    listing = pltpu.make_async_copy(lists, where, list_sem)
    listing.start()
    load.wait()

    def first(c, x, count):
        d = diff[c]
        shape = (count * 80, CZ)
        v = ext[c, pl.ds(x, count)].reshape(shape)
        near = ext[c, pl.ds(x - 1, count)].reshape(shape) + ext[c, pl.ds(x + 1, count)].reshape(shape)
        near = near + pltpu.roll(v, 1, 0) + pltpu.roll(v, shape[0] - 1, 0)
        near = near + jnp.dot(
            jnp.concatenate(split(v), axis=1), taps[...], preferred_element_type=F32
        )
        mid[c, pl.ds(x - 1, count)] = (v + d * near).reshape(count, 80, CZ)

    def second(c, x, count):
        d = diff[c]
        shape = (count * 80, CZ)
        v = mid[c, pl.ds(x + 1, count)].reshape(shape)
        near = mid[c, pl.ds(x, count)].reshape(shape) + mid[c, pl.ds(x + 2, count)].reshape(shape)
        near = near + pltpu.roll(v, 1, 0) + pltpu.roll(v, shape[0] - 1, 0)
        near = near + jnp.dot(
            jnp.concatenate(split(v), axis=1), taps[...], preferred_element_type=F32
        )
        new = (v + d * near).reshape(count, 80, CZ)[:, 8 : 8 + CY]
        res[c, pl.ds(x * CY, count * CY)] = new.reshape(count * CY, CZ)

    def clear(ref, xs, ys):
        @pl.loop(0, COMP)
        def _(c):
            ref[c, pl.ds(*xs), pl.ds(*ys), :] = jnp.zeros((xs[1], ys[1], CZ), F32)

    def edges(ref, xs):
        @pl.when(gy == 0)
        def _():
            clear(ref, xs, (0, 8))

        @pl.when(gy == n_gy - 1)
        def _():
            clear(ref, xs, (CY + 8, 8))

    copies[2].wait_recv()
    copies[3].wait_recv()
    edges(ext, (2, CX))

    @pl.loop(0, COMP)
    def _(c):
        first(c, 3, 7)
        first(c, 10, 7)

    edges(mid, (2, CX - 2))

    @pl.loop(0, COMP)
    def _(c):
        second(c, 2, 6)
        second(c, 8, 6)
        pltpu.make_async_copy(
            res.at[c, pl.ds((2) * CY, (CX - 4) * CY)], out.at[c, pl.ds((2) * CY, (CX - 4) * CY)], out_sem.at[c]
        ).start()

    listing.wait()

    @pl.loop(0, EARLY // 8)
    def _(g):
        for r in range(8):
            at = jnp.clip(where[0, g * 8 + r], 0, CH - 1)
            for c in range(COMP):
                hot[g, pl.ds(c * 8 + r, 1), :] = res[c, pl.ds(at, 1), :]
        first_t[g] = hot[g, 72:80, :]

    inv = inverse[...]
    inv = jnp.concatenate([inv, inv], axis=1)

    @pl.loop(0, FLAME_SUB)
    def _(s):
        for t in range(EARLY // 16):
            flame_tile(hot, t, matrix, inv)

    gain[...] = hot[:, 72:80, :] - first_t[...]

    for number in (0, 1, 4, 5, 6, 7):
        copies[number].wait_recv()
    edges(ext, (1, 1))
    edges(ext, (CX + 2, 1))

    @pl.when(gx == 0)
    def _():
        clear(ext, (0, 2), (0, CY + 16))

    @pl.when(gx == n_gx - 1)
    def _():
        clear(ext, (CX + 2, 2), (0, CY + 16))

    @pl.loop(0, COMP)
    def _(c):
        first(c, 1, 2)
        first(c, CX + 1, 2)

    edges(mid, (1, 1))
    edges(mid, (CX, 1))

    @pl.when(gx == 0)
    def _():
        clear(mid, (0, 1), (0, CY + 16))

    @pl.when(gx == n_gx - 1)
    def _():
        clear(mid, (CX + 1, 1), (0, CY + 16))

    @pl.loop(0, COMP)
    def _(c):
        second(c, 0, 2)
        second(c, CX - 2, 2)
        pltpu.make_async_copy(
            res.at[c, pl.ds((0) * CY, (2) * CY)], out.at[c, pl.ds((0) * CY, (2) * CY)], out_sem.at[COMP + c]
        ).start()
        pltpu.make_async_copy(
            res.at[c, pl.ds((CX - 2) * CY, (2) * CY)], out.at[c, pl.ds((CX - 2) * CY, (2) * CY)], out_sem.at[2 * COMP + c]
        ).start()

    for copy in copies:
        copy.wait_send()

    @pl.loop(0, COMP)
    def _(c):
        pltpu.make_async_copy(
            res.at[c, pl.ds((2) * CY, (CX - 4) * CY)], out.at[c, pl.ds((2) * CY, (CX - 4) * CY)], out_sem.at[c]
        ).wait()
        pltpu.make_async_copy(
            res.at[c, pl.ds((0) * CY, (2) * CY)], out.at[c, pl.ds((0) * CY, (2) * CY)], out_sem.at[COMP + c]
        ).wait()
        pltpu.make_async_copy(
            res.at[c, pl.ds((CX - 2) * CY, (2) * CY)], out.at[c, pl.ds((CX - 2) * CY, (2) * CY)], out_sem.at[2 * COMP + c]
        ).wait()


def sigmoid(x):
    return 0.5 * jnp.tanh(0.5 * x) + 0.5


def substep(state, matrix, inverse):
    high, low = split(state)
    r = jnp.dot(matrix, jnp.concatenate([high, low, high], axis=0), preferred_element_type=F32)
    last = state[72:80]
    base = last * inverse[72:80]
    g0 = sigmoid(last)
    g1 = sigmoid(base + g0 * r[240:248])
    g2 = sigmoid(base + g1 * (r[72:80] + g0 * r[248:256]))
    rows = []
    for c in range(COMP):
        at = 8 * c
        inner = r[80 + at : 88 + at] + g0 * r[160 + at : 168 + at]
        rows.append(state[at : at + 8] * inverse[at : at + 8] + g2 * (r[at : at + 8] + g1 * inner))
    return rows


def flame_tile(cur, t, matrix, inv):
    rows = substep(jnp.concatenate([cur[2 * t], cur[2 * t + 1]], axis=1), matrix[...], inv)
    new = jnp.concatenate(rows, axis=0)
    cur[2 * t] = new[:, :CZ]
    cur[2 * t + 1] = new[:, CZ:]


def chem_kernel(
    u2, hot, gain1, matrix, inverse, index1, index2, lists1, lists2,
    out, terms, uv, ov, cur, gain2, in_sem, out_sem,
):
    def fetch(k):
        part = pl.ds(k * CHUNK, CHUNK)
        return pltpu.make_async_copy(u2.at[:, part, :], uv.at[:, part, :], in_sem.at[k])

    for k in range(CH // CHUNK):
        fetch(k).start()
    inv = inverse[...]
    inv = jnp.concatenate([inv, inv], axis=1)

    def cool_tile(t):
        at = [pl.multiple_of(t * 16 + w * 8, 8) for w in range(2)]
        groups = [
            jnp.concatenate([uv[c, pl.ds(a, 8), :] for c in range(COMP)], axis=0) for a in at
        ]
        rows = substep(jnp.concatenate(groups, axis=1), matrix[...], inv)
        for w in range(2):
            for c in range(COMP):
                ov[c, pl.ds(at[w], 8), :] = rows[c][:, w * CZ : (w + 1) * CZ]

    for k in range(CH // CHUNK):
        fetch(k).wait()
    gain2[...] = jnp.zeros_like(gain2)
    number = jnp.clip(index2[2, 0], 0, FMAX)

    def gather(j):
        @pl.loop(0, LATE // 8)
        def _(g):
            for r in range(8):
                at = index2[0, jnp.minimum(j * LATE + g * 8 + r, FMAX - 1)]
                for c in range(COMP):
                    cur[g, pl.ds(c * 8 + r, 1), :] = uv[c, pl.ds(at, 1), :]
            gain2[j * (LATE // 8) + g] = -cur[g, 72:80, :]

    def scatter(j):
        @pl.loop(0, LATE // 8)
        def _(g):
            gain2[j * (LATE // 8) + g] = gain2[j * (LATE // 8) + g] + cur[g, 72:80, :]

        def one(p, carry):
            at = index2[0, j * LATE + p]
            for c in range(COMP):
                ov[c, pl.ds(at, 1), :] = cur[p >> 3, pl.ds(c * 8 + (p & 7), 1), :]
            return carry

        lax.fori_loop(0, jnp.minimum(number - j * LATE, LATE), one, 0)

    gather(0)

    @pl.loop(0, FLAME_SUB)
    def _(s):
        for t in range(LATE // 16):
            flame_tile(cur, t, matrix, inv)
        for t in range(COOL_EACH):
            cool_tile(s * COOL_EACH + t)

    for t in range(FLAME_SUB * COOL_EACH, CH // 16):
        cool_tile(t)
    scatter(0)

    @pl.loop(1, (number + LATE - 1) // LATE)
    def _(j):
        gather(j)

        @pl.loop(0, FLAME_SUB)
        def _(s):
            for t in range(LATE // 16):
                flame_tile(cur, t, matrix, inv)

        scatter(j)

    def early(p, carry):
        at = index1[0, p]
        for c in range(COMP):
            ov[c, pl.ds(at, 1), :] = hot[p >> 3, pl.ds(c * 8 + (p & 7), 1), :]
        return carry

    lax.fori_loop(0, jnp.clip(index1[2, 0], 0, EARLY), early, 0)
    copy = pltpu.make_async_copy(ov, out, out_sem)
    copy.start()

    row = lax.broadcasted_iota(jnp.int32, (64, FMAX), 0)
    owner = jnp.where((row & 7) < 4, (row & 7) * 8 + (row >> 3), -2)
    total = jnp.zeros((64, CZ), F32)
    for lists, values, count in (
        (lists1, gain1[...].reshape(EARLY, CZ), EARLY),
        (lists2, gain2[0 : FMAX // 8].reshape(FMAX, CZ), FMAX),
    ):
        onehot = (owner[:, :count] == lists[1:2, :count]).astype(BF16)
        for part in split(values):
            total = total + jnp.dot(onehot, part, preferred_element_type=F32)
    terms[...] = total.reshape(8, 8, CZ)
    copy.wait()


def heat_kernel(n_gy, terms, out, got, part, back, send, recv):
    gx, gy = lax.axis_index("gx"), lax.axis_index("gy")
    high = n_gy // 8
    plane = gy // 8
    place = gy - 8 * plane
    near = []
    for k in range(1, 8):
        other = place + k
        near.append(jnp.where(other >= 8, other - 8, other))
    far = []
    for k in range(1, high):
        other = plane + k
        far.append(jnp.where(other >= high, other - high, other))
    barrier = pltpu.get_barrier_semaphore()
    for other in near:
        pl.semaphore_signal(
            barrier, inc=1, device_id=(gx, plane * 8 + other), device_id_type=MESH
        )
    for other in far:
        pl.semaphore_signal(
            barrier, inc=1, device_id=(gx, other * 8 + place), device_id_type=MESH
        )
    pl.semaphore_wait(barrier, 7 + high - 1)

    copies = []
    for k, other in enumerate(near):
        copy = pltpu.make_async_remote_copy(
            src_ref=terms.at[other],
            dst_ref=got.at[k],
            send_sem=send.at[k],
            recv_sem=recv.at[k],
            device_id=(gx, plane * 8 + other),
            device_id_type=MESH,
        )
        copy.start()
        copies.append(copy)
    total = terms[place]
    for k, copy in enumerate(copies):
        copy.wait_recv()
        total = total + got[k]
    part[...] = total
    row = lax.broadcasted_iota(jnp.int32, (8, CZ), 0)
    again = []
    for k, other in enumerate(far):
        copy = pltpu.make_async_remote_copy(
            src_ref=part,
            dst_ref=back.at[k],
            send_sem=send.at[7 + k],
            recv_sem=recv.at[7 + k],
            device_id=(gx, other * 8 + place),
            device_id_type=MESH,
        )
        copy.start()
        again.append(copy)
    for k, copy in enumerate(again):
        copy.wait_recv()
        total = total + back[k]
    total = jnp.where(row == plane, total, 0.0)
    total = jnp.sum(jnp.sum(total, axis=0, keepdims=True), axis=1, keepdims=True)
    out[...] = total * (1.0 / math.sqrt(CZ) / math.sqrt(RMAX))
    for copy in copies + again:
        copy.wait_send()


def per_device(n_gx, n_gy, fields, diffusivity, decay_rates, reaction_matrix, owner_index, flame_flag):
    shape = (COMP, CH, CZ)
    dma = pltpu.SemaphoreType.DMA
    as_f32 = lambda *dims: jax.ShapeDtypeStruct(dims, F32)
    as_i32 = lambda *dims: jax.ShapeDtypeStruct(dims, jnp.int32)
    u2, hot, gain, matrix, inverse, lists, late = pl.pallas_call(
        functools.partial(halo_kernel, n_gx, n_gy),
        out_shape=(
            as_f32(*shape),
            as_f32(EARLY // 8, 80, CZ),
            as_f32(EARLY // 8, 8, CZ),
            jax.ShapeDtypeStruct((256, 240), BF16),
            as_f32(80, CZ),
            as_i32(8, FMAX),
            as_i32(8, FMAX),
        ),
        in_specs=[ANY, SMEM, VMEM, SMEM, VMEM, VMEM],
        out_specs=(ANY,) + (VMEM,) * 6,
        scratch_shapes=[
            pltpu.VMEM((COMP, CX + 4, CY + 16, CZ), F32),
            pltpu.VMEM((COMP, CX + 2, CY + 16, CZ), F32),
            pltpu.VMEM(shape, F32),
            pltpu.VMEM((2 * CZ, CZ), BF16),
            pltpu.VMEM((CZ, CZ), F32),
            pltpu.SMEM((8, FMAX), jnp.int32),
            pltpu.VMEM((EARLY // 8, 8, CZ), F32),
            dma,
            dma((8,)),
            dma((8,)),
            dma((3 * COMP,)),
            dma,
        ],
        compiler_params=pltpu.CompilerParams(
            collective_id=0, has_side_effects=True, vmem_limit_bytes=LIMIT
        ),
        name="halo_diffuse",
    )(
        fields, diffusivity, reaction_matrix, decay_rates,
        flame_flag.reshape(8, CZ), owner_index.reshape(8, CZ),
    )
    chunks = -(-FMAX // LATE)
    merged, terms = pl.pallas_call(
        chem_kernel,
        out_shape=(as_f32(*shape), as_f32(8, 8, CZ)),
        in_specs=[ANY, VMEM, VMEM, VMEM, VMEM, SMEM, SMEM, VMEM, VMEM],
        out_specs=(ANY, VMEM),
        scratch_shapes=[
            pltpu.VMEM(shape, F32),
            pltpu.VMEM(shape, F32),
            pltpu.VMEM((LATE // 8, 80, CZ), F32),
            pltpu.VMEM((chunks * (LATE // 8), 8, CZ), F32),
            dma((CH // CHUNK,)),
            dma,
        ],
        compiler_params=pltpu.CompilerParams(vmem_limit_bytes=LIMIT),
        name="chemistry",
    )(u2, hot, gain, matrix, inverse, lists, late, lists, late)
    heat = pl.pallas_call(
        functools.partial(heat_kernel, n_gy),
        out_shape=as_f32(1, 1),
        in_specs=[VMEM],
        out_specs=VMEM,
        scratch_shapes=[
            pltpu.VMEM((7, 8, CZ), F32),
            pltpu.VMEM((8, CZ), F32),
            pltpu.VMEM((n_gy // 8 - 1, 8, CZ), F32),
            dma((7 + n_gy // 8 - 1,)),
            dma((7 + n_gy // 8 - 1,)),
        ],
        compiler_params=pltpu.CompilerParams(
            collective_id=1, has_side_effects=True, vmem_limit_bytes=LIMIT
        ),
        name="owner_sum",
    )(terms)
    return merged.reshape(COMP, CX, CY, CZ), heat


def solution(mesh):
    return jax.shard_map(
        functools.partial(per_device, mesh.shape["gx"], mesh.shape["gy"]),
        mesh=mesh,
        in_specs=(
            P(None, "gx", "gy", None),
            P(),
            P(),
            P(),
            P("gx", "gy", None),
            P("gx", "gy", None),
        ),
        out_specs=(P(None, "gx", "gy", None), P("gx", "gy")),
        check_vma=False,
    )
```

time: 78.6 us -> 62 us (0.79)
  other arithmetic: 7.72 us -> 0 us
  local copies, waits for them, and re-layouts: 5.41 us -> 0 us
  Pallas kernels: 62.3 us -> 59.3 us
    convert_element_type x2 -> x0, local copies, waits for them, and re-layouts: 4.02 us -> none  [per_device(): (stacked[:, None, :, None] * eye[None, :, None, :]).reshape(256, 240)]
    pallas_call x3, Pallas kernels: 62.3 us -> 59.3 us  [the longest x1 31.2 us: per_device(): pl.pallas_call(functools.partial(halo_kernel, n_gx, n_gy), out_shape=(as_...]
    mul x3 -> x0, other arithmetic: 2.13 us -> none  [the longest x1 0.77 us: per_device(): m1 * inv[None, :]]
    reduce_sum x2 -> x0, other arithmetic: 1.52 us -> none  [the longest x1 1.33 us: per_device(): count = jnp.sum(flags).reshape(1)]
    select_n x2 -> x0, other arithmetic: 1.35 us -> none  [the longest x1 0.76 us: per_device(): rank = jnp.where(flags > 0, jnp.cumsum(flags) - flags, -1)]
    another operation x3 -> x0, other arithmetic: 1.03 us -> none
    broadcast_in_dim x3 -> x0, local copies, waits for them, and re-layouts: 0.83 us -> none  [per_device(): inverse = jnp.broadcast_to(jnp.repeat(inv, 8)[:, None], (80, CZ))]
where the time goes in v1:
time: 62 us; the launch traced here: 61.8 us
  Pallas kernels  59.3 us (96%)
  between operations  2.41 us (4%)
    pallas_call x1, Pallas kernels, per_device(): pl.pallas_call(functools.partial(halo_kernel, n_gx, n_gy), out_shape=(as_...  31.2 us
    pallas_call x1, Pallas kernels, per_device(): pl.pallas_call(chem_kernel, out_shape=(as_f32(*shape), as_f32(8, 8, CZ)),...  14.7 us
    pallas_call x1, Pallas kernels, per_device(): pl.pallas_call(functools.partial(heat_kernel, n_gy), out_shape=as_f32(1,...  13.5 us

profile of v1, /device:TPU:1, one launch (start us, length us, event | category | flops | bytes accessed | tf_op | source)
XLA Modules:
  0.0 61.8 jit_solution(13711277432193327535)
XLA Ops:
  0.6 31.2 %halo_diffuse.1 = (f32[10,1024,128]{2,1,0:T(8,128)}, f32[20,80,128]{2,1,0:T(8,128)}, f32[20,8,128]{2,1,0:T(8,128)}, bf16[256,240]{1,0:T(8,128)(2,1)}, f32[80,128...) custom-call(f32[10,16,64,128]{3,2,1,0:T(8,128)} %fields.1, f32[10]{0:T(128)} %diff.1, f32[10,10]{1,0:T(8,128)} %reaction.1, ...), custom_call_target="tpu_custom_call" | custom-call | tf_op jit(solution)/shard_map/halo_diffuse/pallas_call | solution.py:500
  31.8 14.7 %chemistry.1 = (f32[10,1024,128]{2,1,0:T(8,128)}, f32[8,8,128]{2,1,0:T(8,128)}) custom-call(f32[10,1024,128]{2,1,0:T(8,128)} %get-tuple-element.11.u2, f32[20,80,128]{2,1,0:T(8,128)} %get-tuple-element.12.hot, f32[20,8,128]{2,1,0:T(8,128)} %get-tuple-element.13.gain1, bf16[256,240]{1,0:T(8,128)(2,1)} %get-tuple-element.14.matrix, ...), custom_call_target="tpu_custom_call" | custom-call | tf_op jit(solution)/shard_map/chemistry/pallas_call | solution.py:536
  46.5 13.5 %owner_sum.1 = f32[1,1]{1,0:T(1,128)} custom-call(f32[8,8,128]{2,1,0:T(8,128)} %get-tuple-element.19.terms), custom_call_target="tpu_custom_call" | custom-call | tf_op jit(solution)/shard_map/owner_sum/pallas_call | solution.py:552
